TPU v7x, 32 devices: a whole 2x2x4 slice. The times are simulated.
32 devices in a mesh: batch: 8 (over z, y), hidden: 4 (over x, core).
Axes of the slice: x: 2, y: 2, z: 4, core: 2. Of those that a mesh axis runs over, the one named last changes fastest.
Arguments:
- layer_input: float32 [2, 768, 8192], P(None, 'hidden', 'batch'), may hold values from -6 to 6
- gain_first: float32 [768], P('hidden'), may hold values from 0.5 to 1.5
- shift_first: float32 [768], P('hidden'), may hold values from -2 to 2
- weight_in: float32 [768, 3072], P(None, 'hidden'), may hold values from -0.21875 to 0.21875
- bias_in: float32 [3072], P('hidden'), may hold values from -2 to 2
- weight_out: float32 [3072, 768], P('hidden'), may hold values from -0.109375 to 0.109375
- bias_out: float32 [768], P('hidden'), may hold values from -2 to 2
- gain_second: float32 [768], P('hidden'), may hold values from 0.5 to 1.5
- shift_second: float32 [768], P('hidden'), may hold values from -2 to 2
- cotangent: float32 [2, 768, 8192], P(None, 'hidden', 'batch'), may hold values from -6 to 6
- live_counts: int32 [8], P('batch'), may hold values from 1 to 2, as said below
Outputs:
- layer_output: float32 [2, 768, 8192], P(None, 'hidden', 'batch')
- input_grad: float32 [2, 768, 8192], P(None, 'hidden', 'batch')
- gain_first_grad: float32 [768], P('hidden')
- shift_first_grad: float32 [768], P('hidden')
- weight_in_grad: float32 [768, 3072], P(None, 'hidden')
- bias_in_grad: float32 [3072], P('hidden')
- weight_out_grad: float32 [3072, 768], P('hidden')
- bias_out_grad: float32 [768], P('hidden')
- gain_second_grad: float32 [768], P('hidden')
- shift_second_grad: float32 [768], P('hidden')
Inputs may be any that keep to these rules, and one draw needn't show every extreme that they name: `live_counts`: entries are equal within each aligned block of 4 batch indices (one batch group); each group holds 1 to 2 live sequences in its first slots; some group has all 2 slots live.
All inputs are finite; a program needn't handle non-finite values.
Results may differ from a plain program's by a relative error of at most 0.008.
Values may be sent and summed in bfloat16 or wider, within the bound.
A program may use at most 128 MiB of HBM per device.

v0:
```python
import math

import jax
import jax.numpy as jnp
from jax import lax
from jax.sharding import PartitionSpec as P

SPLIT = 4


EPS = 1e-06


def from_partner(block, axis, bit):
    count = lax.axis_size(axis)
    route = []
    for low in range(count):
        high = low | 1 << bit
        if high != low and high < count:
            route += [(low, high), (high, low)]
    return lax.ppermute(block, axis, route)


def dft_tables(count, first, rows):
    index = first + jnp.arange(rows, dtype=jnp.int32)
    column = jnp.arange(count, dtype=jnp.int32)
    phase = index[:, None] * column[None, :] % count
    angle = phase.astype(jnp.float32) * (2.0 * math.pi / count)
    factor = 1.0 / math.sqrt(count)
    return (
        (jnp.cos(angle) * factor).astype(jnp.bfloat16),
        (jnp.sin(angle) * factor).astype(jnp.bfloat16),
    )


def product(left, right):
    return jnp.dot(left, right, preferred_element_type=jnp.float32)


def product_left(left, right):
    return lax.dot_general(
        left, right, (((0,), (0,)), ((), ())), preferred_element_type=jnp.float32
    )


def product_right(left, right):
    return lax.dot_general(
        left, right, (((1,), (1,)), ((), ())), preferred_element_type=jnp.float32
    )


def collect(piece, sender, position):
    gathered = piece
    for bit in range(SPLIT.bit_length() - 1):
        other = sender(gathered, bit)
        upper = position >> bit & 1 == 1
        gathered = jnp.where(
            upper, jnp.concatenate((other, gathered), -1), jnp.concatenate((gathered, other), -1)
        )
    return gathered


def row_sums(first, second):
    return lax.psum((jnp.sum(first, 0, keepdims=True), jnp.sum(second, 0, keepdims=True)), "hidden")


def normalize(resid, gain, shift, width):
    total, squares = row_sums(resid, resid * resid)
    average = total / width
    variance = squares / width - average * average
    inverse = lax.rsqrt(variance + EPS)
    unit = (resid - average) * inverse
    return (unit * gain[:, None] + shift[:, None], unit, inverse)


def norm_back(grad, unit, inverse, gain, width):
    scaled = grad * gain[:, None]
    total, cross = row_sums(scaled, scaled * unit)
    return inverse * (scaled - total / width - unit * cross / width)


def local(
    layer_input,
    gain_first,
    shift_first,
    weight_in,
    bias_in,
    weight_out,
    bias_out,
    gain_second,
    shift_second,
    cotangent,
    live_counts,
):
    slots, part_width, piece_len = layer_input.shape
    width = part_width * lax.axis_size("hidden")
    offset = lax.axis_index("hidden") * part_width
    position = lax.axis_index("batch") % SPLIT
    seq_len = piece_len * SPLIT
    cos_seq, sin_seq = dft_tables(seq_len, position * piece_len, piece_len)
    cos_hid, sin_hid = dft_tables(width, offset, part_width)
    w_in = weight_in.astype(jnp.bfloat16)
    w_out = weight_out.astype(jnp.bfloat16)
    grads_init = (
        jnp.zeros_like(gain_first),
        jnp.zeros_like(shift_first),
        jnp.zeros_like(weight_in),
        jnp.zeros_like(bias_in),
        jnp.zeros_like(weight_out),
        jnp.zeros_like(bias_out),
        jnp.zeros_like(gain_second),
        jnp.zeros_like(shift_second),
    )

    def one_slot(slot_index, running):
        outputs, in_grads, grads = running
        live_flag = (slot_index < live_counts[0]).astype(jnp.float32)
        values = lax.dynamic_index_in_dim(layer_input, slot_index, 0, keepdims=False)
        grad_out = lax.dynamic_index_in_dim(cotangent, slot_index, 0, keepdims=False) * live_flag
        rounded = values.astype(jnp.bfloat16)
        whole = collect(rounded, lambda block, bit: from_partner(block, "batch", bit), position)
        spec_cos = product_right(whole, cos_seq).astype(jnp.bfloat16)
        spec_sin = product_right(whole, sin_seq).astype(jnp.bfloat16)
        partial_value = product_left(cos_hid, spec_cos) - product_left(sin_hid, spec_sin)
        mixed = lax.psum_scatter(partial_value, "hidden", scatter_dimension=0, tiled=True)
        first, unit_first, inverse_first = normalize(values + mixed, gain_first, shift_first, width)
        first_full = lax.all_gather(first.astype(jnp.bfloat16), "hidden", axis=0, tiled=True)
        before = product_left(w_in, first_full) + bias_in[:, None]
        hidden, gelu_pull = jax.vjp(lambda inner: jax.nn.gelu(inner, approximate=True), before)
        hidden_low = hidden.astype(jnp.bfloat16)
        branch = (
            lax.psum_scatter(
                product_left(w_out, hidden_low), "hidden", scatter_dimension=0, tiled=True
            )
            + bias_out[:, None]
        )
        second, unit_second, inverse_second = normalize(
            first + branch, gain_second, shift_second, width
        )
        grad_second = norm_back(grad_out, unit_second, inverse_second, gain_second, width)
        grad_full = lax.all_gather(grad_second.astype(jnp.bfloat16), "hidden", axis=0, tiled=True)
        grad_hidden = product(w_out, grad_full)
        grad_before = gelu_pull(grad_hidden)[0]
        grad_before_low = grad_before.astype(jnp.bfloat16)
        back_partial = product(w_in, grad_before_low)
        grad_first = grad_second + lax.psum_scatter(
            back_partial, "hidden", scatter_dimension=0, tiled=True
        )
        grad_mix = norm_back(grad_first, unit_first, inverse_first, gain_first, width)
        grad_mix_low = grad_mix.astype(jnp.bfloat16)
        grad_mix_full = lax.all_gather(grad_mix_low, "hidden", axis=0, tiled=True)
        grad_cos = product(cos_hid, grad_mix_full)
        grad_sin = -product(sin_hid, grad_mix_full)
        stacked = jnp.stack((grad_cos.astype(jnp.bfloat16), grad_sin.astype(jnp.bfloat16)))
        spread = collect(stacked, lambda block, bit: from_partner(block, "batch", bit), position)
        grad_values = (
            grad_mix + product_right(spread[0], cos_seq) + product_right(spread[1], sin_seq)
        )
        updates = (
            jnp.sum(grad_first * unit_first, 1),
            jnp.sum(grad_first, 1),
            product_right(first_full, grad_before_low),
            jnp.sum(grad_before, 1),
            product_right(hidden_low, grad_full),
            jnp.sum(grad_second, 1),
            jnp.sum(grad_out * unit_second, 1),
            jnp.sum(grad_out, 1),
        )
        grads = tuple((older + newer for older, newer in zip(grads, updates)))
        outputs = lax.dynamic_update_index_in_dim(outputs, second * live_flag, slot_index, 0)
        in_grads = lax.dynamic_update_index_in_dim(in_grads, grad_values, slot_index, 0)
        return (outputs, in_grads, grads)

    outputs, in_grads, grads = lax.fori_loop(
        0, slots, one_slot, (jnp.zeros_like(layer_input), jnp.zeros_like(layer_input), grads_init)
    )
    summed = lax.psum(
        (grads[0], grads[1], grads[2], grads[3], grads[4], grads[5], grads[6], grads[7]), "batch"
    )
    return (
        outputs,
        in_grads,
        summed[0],
        summed[1],
        summed[2],
        summed[3],
        summed[4],
        summed[5],
        summed[6],
        summed[7],
    )


def solution(mesh):
    return jax.shard_map(
        local,
        mesh=mesh,
        in_specs=(
            P(None, "hidden", "batch"),
            P("hidden"),
            P("hidden"),
            P(None, "hidden"),
            P("hidden"),
            P("hidden", None),
            P("hidden"),
            P("hidden"),
            P("hidden"),
            P(None, "hidden", "batch"),
            P("batch"),
        ),
        out_specs=(
            P(None, "hidden", "batch"),
            P(None, "hidden", "batch"),
            P("hidden"),
            P("hidden"),
            P(None, "hidden"),
            P("hidden"),
            P("hidden", None),
            P("hidden"),
            P("hidden"),
            P("hidden"),
        ),
        check_vma=False,
    )
```

profile of v0, /device:TPU:0, one launch (start us, length us, event | category | flops | bytes accessed | tf_op | source)
XLA Modules:
  0.0 1414.9 jit_solution(18446456711246053054)
XLA Ops:
  8.2 2.9 convert_element_type.146
  12.4 1215.4 %while.36 = (s32[]{:T(128)}, f32[2,192,1024]{2,1,0:T(8,128)}, f32[2,192,1024]{2,1,0:T(8,128)}, f32[192]{0:T(256)S(1)}, f32[192]{0:T(256)S(1)}, /*index=5*/f32[76...) while((s32[]{:T(128)}, f32[2,192,1024]{2,1,0:T(8,128)}, ...), condition=%wide.region_26.27_spmd.clone.clone.clone, body=%wide.region_0.26_spmd.clone.clone.clone.sunk | while | flops 15267280896 | bytes 303473984 | solution.py:174
  13.9 3.0 collective-permute-start
  16.9 9.1 collective-permute-done
  33.0 12.0 collective-permute-done.1
  45.1 67.7 %fusion.171 = f32[1024,768]{1,0:T(8,128)} fusion(s32[1024]{0:T(1024)S(1)} %get-tuple-element.1306, bf16[192,2048]{1,0:T(8,128)(2,1)S(1)} %maximum_select_fusion.21, bf16[192,2048]{1,0:T(8,128)(2,1)S(1)} %collective-permute-done.1, pred[]{:T(512)} %get-tuple-element.1294, bf16[192,768]{1,0:T(8,128)(2,1)S(1)} %multiply_convert_fusion.62), kind=kOutput, calls=%fused_computation.53.clone.3 | convolution fusion | flops 1986985984 | bytes 5017601 | tf_op jit(solution)/shard_map/while/body/eval_jaxpr/dot_general | solution.py:41
  112.8 69.3 %subtract_bitcast_fusion.2 = f32[768,1024]{0,1:T(8,128)} fusion(f32[1024,768]{1,0:T(8,128)} %fusion.171, s32[1024]{0:T(1024)S(1)} %get-tuple-element.1306, bf16[192,2048]{1,0:T(8,128)(2,1)S(1)} %maximum_select_fusion.21, bf16[192,2048]{1,0:T(8,128)(2,1)S(1)} %collective-permute-done.1, pred[]{:T(512)} %get-tuple-element.1294, ...), kind=kOutput, calls=%fused_computation.35.clone.3 | convolution fusion | flops 1987772416 | bytes 8163329 | tf_op jit(solution)/shard_map/while/body/eval_jaxpr/dot_general | solution.py:41
  182.1 3.6 copy.39
  185.7 39.2 %reduce-scatter.16.cloned.1.call-done = f32[192,1024]{1,0:T(8,128)} async-done(((f32[768,1024]{1,0:T(8,128)}), f32[192,1024]{1,0:T(8,128)}) %reduce-scatter.16.cloned.1.call-update) | async-done | bytes 786448 | tf_op jit(solution)/shard_map/while/body/eval_jaxpr/reduce_scatter | solution.py:125
  226.5 5.9 all-reduce.10
  233.4 20.9 %all-gather.4.cloned.1.call-done = bf16[768,1024]{1,0:T(8,128)(2,1)} async-done(((bf16[192,1024]{1,0:T(8,128)(2,1)}), bf16[768,1024]{1,0:T(8,128)(2,1)}) %all-gather.4.cloned.1.call-update) | async-done | bytes 1572880 | tf_op jit(solution)/shard_map/while/body/eval_jaxpr/all_gather | solution.py:127
  254.3 2.9 fusion.174
  259.0 3.8 convolution_bitcast_fusion.4
  262.8 3.6 copy.40
  267.1 37.4 %reduce-scatter.18.cloned.1.call-done = f32[192,1024]{1,0:T(8,128)} async-done(((f32[768,1024]{1,0:T(8,128)}), f32[192,1024]{1,0:T(8,128)}) %reduce-scatter.18.cloned.1.call-update) | async-done | bytes 786448 | tf_op jit(solution)/shard_map/while/body/eval_jaxpr/reduce_scatter | solution.py:132
  305.9 5.9 all-reduce.11
  313.2 5.8 all-reduce.12
  321.5 21.3 %all-gather.6.cloned.1.call-done = bf16[768,1024]{1,0:T(8,128)(2,1)} async-done(((bf16[192,1024]{1,0:T(8,128)(2,1)}), bf16[768,1024]{1,0:T(8,128)(2,1)}) %all-gather.6.cloned.1.call-update) | async-done | bytes 1572880 | tf_op jit(solution)/shard_map/while/body/eval_jaxpr/all_gather | solution.py:141
  342.8 6.1 fusion.178
  350.0 4.4 convolution_bitcast_fusion.5
  354.4 3.6 copy.41
  358.1 38.0 %reduce-scatter.20.cloned.1.call-done = f32[192,1024]{1,0:T(8,128)} async-done(((f32[768,1024]{1,0:T(8,128)}), f32[192,1024]{1,0:T(8,128)}) %reduce-scatter.20.cloned.1.call-update) | async-done | bytes 786448 | tf_op jit(solution)/shard_map/while/body/eval_jaxpr/reduce_scatter | solution.py:146
  397.7 6.0 all-reduce.13
  406.0 19.7 %all-gather.8.cloned.1.call-done = bf16[768,1024]{1,0:T(8,128)(2,1)} async-done(((bf16[192,1024]{1,0:T(8,128)(2,1)}), bf16[768,1024]{1,0:T(8,128)(2,1)}) %all-gather.8.cloned.1.call-update) | async-done | bytes 1572880 | tf_op jit(solution)/shard_map/while/body/eval_jaxpr/all_gather | solution.py:151
  425.7 4.2 fusion.181
  429.9 3.4 fusion.180
  436.9 17.4 %collective-permute-done.2 = bf16[2,192,1024]{2,1,0:T(8,128)(2,1)} collective-permute-done((bf16[2,192,1024]{2,1,0:T(8,128)(2,1)}, bf16[2,192,1024]{2,1,0:T(8,128)(2,1)}, u32[]{:S(2)}, u32[]{:S(2)}) %collective-permute-start.2) | collective-permute-done | bytes 786464 | tf_op jit(solution)/shard_map/while/body/eval_jaxpr/ppermute | solution.py:21
  457.8 3.6 select_add_fusion.16
  461.4 2.9 select_add_fusion.18
  464.4 27.6 %collective-permute-done.3 = bf16[2,192,2048]{2,1,0:T(8,128)(2,1)S(1)} collective-permute-done((bf16[2,192,2048]{2,1,0:T(8,128)(2,1)S(1)}, bf16[2,192,2048]{2,1,0:T(8,128)(2,1)S(1)}, u32[]{:S(2)}, u32[]{:S(2)}) %collective-permute-start.3) | collective-permute-done | bytes 1572896 | tf_op jit(solution)/shard_map/while/body/eval_jaxpr/ppermute | solution.py:21
  493.4 64.2 %fusion.182 = f32[192,1024]{1,0:T(8,128)S(1)} fusion(s32[1024]{0:T(1024)S(1)} %get-tuple-element.1306, bf16[192,4096]{1,0:T(8,128)(2,1)S(1)} %slice_bitcast_fusion.22), kind=kOutput, calls=%fused_computation.17.clone.3 | convolution fusion | flops 1677721600 | bytes 2363392 | tf_op jit(solution)/shard_map/while/body/eval_jaxpr/dot_general | solution.py:47
  557.7 63.3 %fusion.183 = f32[2,192,1024]{2,1,0:T(8,128)S(1)} fusion(f32[2,192,1024]{2,1,0:T(8,128)S(1)} %copy-done.17, s32[]{:T(128)S(6)} %copy.55, f32[192,1024]{1,0:T(8,128)S(1)} %fusion.182, s32[1024]{0:T(1024)S(1)} %get-tuple-element.1306, f32[1024]{0:T(1024)S(1)} %get-tuple-element.1216, f32[192,1024]{1,0:T(8,128)S(1)} %get-tuple-element.1194, ...), kind=kOutput, calls=%fused_computation.48.clone.3 | convolution fusion | flops 1679687680 | bytes 4740100 | tf_op jit(solution)/shard_map/while/body/eval_jaxpr/dot_general | solution.py:47
  625.3 8.0 collective-permute-done
  640.1 10.6 collective-permute-done.1
  650.7 67.3 %fusion.171 = f32[1024,768]{1,0:T(8,128)} fusion(s32[1024]{0:T(1024)S(1)} %get-tuple-element.1306, bf16[192,2048]{1,0:T(8,128)(2,1)S(1)} %maximum_select_fusion.21, bf16[192,2048]{1,0:T(8,128)(2,1)S(1)} %collective-permute-done.1, pred[]{:T(512)} %get-tuple-element.1294, bf16[192,768]{1,0:T(8,128)(2,1)S(1)} %multiply_convert_fusion.62), kind=kOutput, calls=%fused_computation.53.clone.3 | convolution fusion | flops 1986985984 | bytes 5017601 | tf_op jit(solution)/shard_map/while/body/eval_jaxpr/dot_general | solution.py:41
  718.0 69.3 %subtract_bitcast_fusion.2 = f32[768,1024]{0,1:T(8,128)} fusion(f32[1024,768]{1,0:T(8,128)} %fusion.171, s32[1024]{0:T(1024)S(1)} %get-tuple-element.1306, bf16[192,2048]{1,0:T(8,128)(2,1)S(1)} %maximum_select_fusion.21, bf16[192,2048]{1,0:T(8,128)(2,1)S(1)} %collective-permute-done.1, pred[]{:T(512)} %get-tuple-element.1294, ...), kind=kOutput, calls=%fused_computation.35.clone.3 | convolution fusion | flops 1987772416 | bytes 8163329 | tf_op jit(solution)/shard_map/while/body/eval_jaxpr/dot_general | solution.py:41
  787.3 3.6 copy.39
  791.0 38.1 %reduce-scatter.16.cloned.1.call-done = f32[192,1024]{1,0:T(8,128)} async-done(((f32[768,1024]{1,0:T(8,128)}), f32[192,1024]{1,0:T(8,128)}) %reduce-scatter.16.cloned.1.call-update) | async-done | bytes 786448 | tf_op jit(solution)/shard_map/while/body/eval_jaxpr/reduce_scatter | solution.py:125
  830.6 5.9 all-reduce.10
  837.6 20.9 %all-gather.4.cloned.1.call-done = bf16[768,1024]{1,0:T(8,128)(2,1)} async-done(((bf16[192,1024]{1,0:T(8,128)(2,1)}), bf16[768,1024]{1,0:T(8,128)(2,1)}) %all-gather.4.cloned.1.call-update) | async-done | bytes 1572880 | tf_op jit(solution)/shard_map/while/body/eval_jaxpr/all_gather | solution.py:127
  858.5 2.9 fusion.174
  863.1 3.8 convolution_bitcast_fusion.4
  866.9 3.6 copy.40
  871.2 37.4 %reduce-scatter.18.cloned.1.call-done = f32[192,1024]{1,0:T(8,128)} async-done(((f32[768,1024]{1,0:T(8,128)}), f32[192,1024]{1,0:T(8,128)}) %reduce-scatter.18.cloned.1.call-update) | async-done | bytes 786448 | tf_op jit(solution)/shard_map/while/body/eval_jaxpr/reduce_scatter | solution.py:132
  910.0 5.9 all-reduce.11
  917.4 5.8 all-reduce.12
  925.6 21.2 %all-gather.6.cloned.1.call-done = bf16[768,1024]{1,0:T(8,128)(2,1)} async-done(((bf16[192,1024]{1,0:T(8,128)(2,1)}), bf16[768,1024]{1,0:T(8,128)(2,1)}) %all-gather.6.cloned.1.call-update) | async-done | bytes 1572880 | tf_op jit(solution)/shard_map/while/body/eval_jaxpr/all_gather | solution.py:141
  946.9 6.1 fusion.178
  954.2 4.4 convolution_bitcast_fusion.5
  958.6 3.6 copy.41
  962.2 38.1 %reduce-scatter.20.cloned.1.call-done = f32[192,1024]{1,0:T(8,128)} async-done(((f32[768,1024]{1,0:T(8,128)}), f32[192,1024]{1,0:T(8,128)}) %reduce-scatter.20.cloned.1.call-update) | async-done | bytes 786448 | tf_op jit(solution)/shard_map/while/body/eval_jaxpr/reduce_scatter | solution.py:146
  1001.8 6.3 all-reduce.13
  1010.4 19.7 %all-gather.8.cloned.1.call-done = bf16[768,1024]{1,0:T(8,128)(2,1)} async-done(((bf16[192,1024]{1,0:T(8,128)(2,1)}), bf16[768,1024]{1,0:T(8,128)(2,1)}) %all-gather.8.cloned.1.call-update) | async-done | bytes 1572880 | tf_op jit(solution)/shard_map/while/body/eval_jaxpr/all_gather | solution.py:151
  1030.1 4.2 fusion.181
  1034.3 3.4 fusion.180
  1041.2 17.4 %collective-permute-done.2 = bf16[2,192,1024]{2,1,0:T(8,128)(2,1)} collective-permute-done((bf16[2,192,1024]{2,1,0:T(8,128)(2,1)}, bf16[2,192,1024]{2,1,0:T(8,128)(2,1)}, u32[]{:S(2)}, u32[]{:S(2)}) %collective-permute-start.2) | collective-permute-done | bytes 786464 | tf_op jit(solution)/shard_map/while/body/eval_jaxpr/ppermute | solution.py:21
  1062.2 3.6 select_add_fusion.16
  1065.8 2.9 select_add_fusion.18
  1068.8 27.6 %collective-permute-done.3 = bf16[2,192,2048]{2,1,0:T(8,128)(2,1)S(1)} collective-permute-done((bf16[2,192,2048]{2,1,0:T(8,128)(2,1)S(1)}, bf16[2,192,2048]{2,1,0:T(8,128)(2,1)S(1)}, u32[]{:S(2)}, u32[]{:S(2)}) %collective-permute-start.3) | collective-permute-done | bytes 1572896 | tf_op jit(solution)/shard_map/while/body/eval_jaxpr/ppermute | solution.py:21
  1097.8 64.2 %fusion.182 = f32[192,1024]{1,0:T(8,128)S(1)} fusion(s32[1024]{0:T(1024)S(1)} %get-tuple-element.1306, bf16[192,4096]{1,0:T(8,128)(2,1)S(1)} %slice_bitcast_fusion.22), kind=kOutput, calls=%fused_computation.17.clone.3 | convolution fusion | flops 1677721600 | bytes 2363392 | tf_op jit(solution)/shard_map/while/body/eval_jaxpr/dot_general | solution.py:47
  1162.1 63.3 %fusion.183 = f32[2,192,1024]{2,1,0:T(8,128)S(1)} fusion(f32[2,192,1024]{2,1,0:T(8,128)S(1)} %copy-done.17, s32[]{:T(128)S(6)} %copy.55, f32[192,1024]{1,0:T(8,128)S(1)} %fusion.182, s32[1024]{0:T(1024)S(1)} %get-tuple-element.1306, f32[1024]{0:T(1024)S(1)} %get-tuple-element.1216, f32[192,1024]{1,0:T(8,128)S(1)} %get-tuple-element.1194, ...), kind=kOutput, calls=%fused_computation.48.clone.3 | convolution fusion | flops 1679687680 | bytes 4740100 | tf_op jit(solution)/shard_map/while/body/eval_jaxpr/dot_general | solution.py:47
  1228.4 23.2 %all-reduce.4 = (f32[192]{0:T(256)}, f32[192]{0:T(256)}, f32[768]{0:T(1024)}, f32[192]{0:T(256)}, f32[192]{0:T(256)}, /*index=5*/f32[192]{0:T(256)}) all-reduce(f32[192]{0:T(256)S(1)} %get-tuple-element.648, f32[192]{0:T(256)S(1)} %get-tuple-element.649, ...), channel_id=1, replica_groups=mesh['batch'=8,'hidden'=4] {'batch'}, use_global_device_ids=true, to_apply=%region_27.28 | all-reduce | flops 1728 | bytes 13824 | tf_op jit(solution)/shard_map/psum | solution.py:177
  1251.6 150.8 %all-reduce.16.cloned.1.call-done = (f32[768,768]{1,0:T(8,128)}, f32[768,768]{1,0:T(8,128)}) async-done(((f32[768,768]{1,0:T(8,128)}, f32[768,768]{1,0:T(8,128)}), (f32[768,768]{1,0:T(8,128)}, f32[768,768]{1,0:T(8,128)})) %all-reduce.16.cloned.1.call-update) | async-done | bytes 4718608 | tf_op jit(solution)/shard_map/psum | solution.py:177
  1402.4 3.4 copy.79
  (175 shorter events, 69.9 us)
Async XLA Ops:
  8.0 3.2 copy-start
  8.2 4.2 copy-start.8
  8.2 4.2 copy-start.9
  8.2 4.2 copy-start.10
  8.2 4.1 copy-start.11
  8.2 4.1 copy-start.12
  8.2 4.1 copy-start.16
  12.6 212.3 %reduce-scatter.16.cloned.1.call-start = ((), (), s32[]{:S(2)}) async-start(), calls=%async_computation.4 | async-start | bytes 3932160 | tf_op jit(solution)/shard_map/while/body/eval_jaxpr/reduce_scatter | solution.py:125
  13.9 12.1 collective-permute-start
  26.3 18.8 %collective-permute-start.1 = (bf16[192,2048]{1,0:T(8,128)(2,1)S(1)}, bf16[192,2048]{1,0:T(8,128)(2,1)S(1)}, u32[]{:S(2)}, u32[]{:S(2)}) collective-permute-start(bf16[192,2048]{1,0:T(8,128)(2,1)S(1)} %maximum_select_fusion.21), channel_id=1, source_target_pairs={{0,8},{8,0},{4,12},{12,4},{16,24},{24,16},{20,28},{28,20},{1,9},{9... | collective-permute-start | bytes 2359304 | tf_op jit(solution)/shard_map/while/body/eval_jaxpr/ppermute | solution.py:21
  185.7 68.7 %copy-start.6 = (bf16[768,768]{1,0:T(8,128)(2,1)S(1)}, bf16[768,768]{1,0:T(8,128)(2,1)}, u32[]{:S(2)}) copy-start(bf16[768,768]{1,0:T(8,128)(2,1)} %get-tuple-element.1298) | copy-start | bytes 3538948 | tf_op jit(solution)/shard_map/while
  185.7 68.7 %all-gather.4.cloned.1.call-start = ((), (), s32[]{:S(2)}) async-start(), calls=%async_computation.5 | async-start | bytes 1966080 | tf_op jit(solution)/shard_map/while/body/eval_jaxpr/all_gather | solution.py:127
  233.4 71.1 %reduce-scatter.18.cloned.1.call-start = ((), (), s32[]{:S(2)}) async-start(), calls=%async_computation.6 | async-start | bytes 3932160 | tf_op jit(solution)/shard_map/while/body/eval_jaxpr/reduce_scatter | solution.py:132
  254.3 4.6 copy-start.7
  257.3 1.7 copy-start.19
  266.4 76.4 %all-gather.6.cloned.1.call-start = ((), (), s32[]{:S(2)}) async-start(), calls=%async_computation.7 | async-start | bytes 1966080 | tf_op jit(solution)/shard_map/while/body/eval_jaxpr/all_gather | solution.py:141
  321.4 74.7 %reduce-scatter.20.cloned.1.call-start = ((), (), s32[]{:S(2)}) async-start(), calls=%async_computation.8 | async-start | bytes 3932160 | tf_op jit(solution)/shard_map/while/body/eval_jaxpr/reduce_scatter | solution.py:146
  348.8 1.2 copy-start.21
  358.0 67.6 %all-gather.8.cloned.1.call-start = ((), (), s32[]{:S(2)}) async-start(), calls=%async_computation.9 | async-start | bytes 1966080 | tf_op jit(solution)/shard_map/while/body/eval_jaxpr/all_gather | solution.py:151
  425.7 4.2 copy-start.15
  434.2 20.0 %collective-permute-start.2 = (bf16[2,192,1024]{2,1,0:T(8,128)(2,1)}, bf16[2,192,1024]{2,1,0:T(8,128)(2,1)}, u32[]{:S(2)}, u32[]{:S(2)}) collective-permute-start(bf16[2,192,1024]{2,1,0:T(8,128)(2,1)} %pad_maximum_fusion.2), channel_id=1, source_target_pairs={{0,4},{4,0},{8,12},{12,8},{16,20},{20,16},{24,28},{28,24},{1,5},{5... | collective-permute-start | bytes 2359304 | tf_op jit(solution)/shard_map/while/body/eval_jaxpr/ppermute | solution.py:21
  435.7 22.1 %copy-start.3 = (f32[768,768]{1,0:T(8,128)S(1)}, f32[768,768]{1,0:T(8,128)}, u32[]{:S(2)}) copy-start(f32[768,768]{1,0:T(8,128)} %get-tuple-element.1259) | copy-start | bytes 7077892 | tf_op jit(solution)/shard_map/while
  435.7 22.1 %copy-start.13 = (bf16[768,1024]{1,0:T(8,128)(2,1)S(1)}, bf16[768,1024]{1,0:T(8,128)(2,1)}, u32[]{:S(2)}) copy-start(bf16[768,1024]{1,0:T(8,128)(2,1)} %all-gather.4.cloned.1.call-done) | copy-start | bytes 4718596 | tf_op jit(solution)/shard_map/while
  456.2 35.8 %collective-permute-start.3 = (bf16[2,192,2048]{2,1,0:T(8,128)(2,1)S(1)}, bf16[2,192,2048]{2,1,0:T(8,128)(2,1)S(1)}, u32[]{:S(2)}, u32[]{:S(2)}) collective-permute-start(bf16[2,192,2048]{2,1,0:T(8,128)(2,1)S(1)} %maximum_select_fusion.22), channel_id=1, source_target_pairs={{0,8},{8,0},{4,12},{12,4},{16,24},{24,16},{20,28},{28,20},{1,9},{9... | collective-permute-start | bytes 4718600 | tf_op jit(solution)/shard_map/while/body/eval_jaxpr/ppermute | solution.py:21
  457.8 3.6 copy-start.1
  457.8 3.6 copy-start.14
  457.8 3.6 copy-start.20
  461.4 3.0 copy-start.4
  464.4 28.8 %copy-start.2 = (f32[768,768]{1,0:T(8,128)}, f32[768,768]{1,0:T(8,128)S(1)}, u32[]{:S(2)}) copy-start(f32[768,768]{1,0:T(8,128)S(1)} %select_add_fusion.18) | copy-start | bytes 7077892 | tf_op jit(solution)/shard_map/while
  493.4 64.3 %copy-start.17 = (f32[2,192,1024]{2,1,0:T(8,128)S(1)}, f32[2,192,1024]{2,1,0:T(8,128)}, u32[]{:S(2)}) copy-start(f32[2,192,1024]{2,1,0:T(8,128)} %get-tuple-element.1256) | copy-start | bytes 4718596 | tf_op jit(solution)/shard_map/while
  621.0 1.1 copy-start.18
  622.6 206.5 %reduce-scatter.16.cloned.1.call-start = ((), (), s32[]{:S(2)}) async-start(), calls=%async_computation.4 | async-start | bytes 3932160 | tf_op jit(solution)/shard_map/while/body/eval_jaxpr/reduce_scatter | solution.py:125
  623.8 9.6 collective-permute-start
  633.6 17.1 %collective-permute-start.1 = (bf16[192,2048]{1,0:T(8,128)(2,1)S(1)}, bf16[192,2048]{1,0:T(8,128)(2,1)S(1)}, u32[]{:S(2)}, u32[]{:S(2)}) collective-permute-start(bf16[192,2048]{1,0:T(8,128)(2,1)S(1)} %maximum_select_fusion.21), channel_id=1, source_target_pairs={{0,8},{8,0},{4,12},{12,4},{16,24},{24,16},{20,28},{28,20},{1,9},{9... | collective-permute-start | bytes 2359304 | tf_op jit(solution)/shard_map/while/body/eval_jaxpr/ppermute | solution.py:21
  790.9 67.6 %copy-start.6 = (bf16[768,768]{1,0:T(8,128)(2,1)S(1)}, bf16[768,768]{1,0:T(8,128)(2,1)}, u32[]{:S(2)}) copy-start(bf16[768,768]{1,0:T(8,128)(2,1)} %get-tuple-element.1298) | copy-start | bytes 3538948 | tf_op jit(solution)/shard_map/while
  790.9 67.5 %all-gather.4.cloned.1.call-start = ((), (), s32[]{:S(2)}) async-start(), calls=%async_computation.5 | async-start | bytes 1966080 | tf_op jit(solution)/shard_map/while/body/eval_jaxpr/all_gather | solution.py:127
  837.5 71.1 %reduce-scatter.18.cloned.1.call-start = ((), (), s32[]{:S(2)}) async-start(), calls=%async_computation.6 | async-start | bytes 3932160 | tf_op jit(solution)/shard_map/while/body/eval_jaxpr/reduce_scatter | solution.py:132
  858.5 4.6 copy-start.7
  861.4 1.7 copy-start.19
  870.5 76.4 %all-gather.6.cloned.1.call-start = ((), (), s32[]{:S(2)}) async-start(), calls=%async_computation.7 | async-start | bytes 1966080 | tf_op jit(solution)/shard_map/while/body/eval_jaxpr/all_gather | solution.py:141
  925.6 74.7 %reduce-scatter.20.cloned.1.call-start = ((), (), s32[]{:S(2)}) async-start(), calls=%async_computation.8 | async-start | bytes 3932160 | tf_op jit(solution)/shard_map/while/body/eval_jaxpr/reduce_scatter | solution.py:146
  953.0 1.2 copy-start.21
  962.2 67.9 %all-gather.8.cloned.1.call-start = ((), (), s32[]{:S(2)}) async-start(), calls=%async_computation.9 | async-start | bytes 1966080 | tf_op jit(solution)/shard_map/while/body/eval_jaxpr/all_gather | solution.py:151
  1030.1 4.2 copy-start.15
  1038.6 20.0 %collective-permute-start.2 = (bf16[2,192,1024]{2,1,0:T(8,128)(2,1)}, bf16[2,192,1024]{2,1,0:T(8,128)(2,1)}, u32[]{:S(2)}, u32[]{:S(2)}) collective-permute-start(bf16[2,192,1024]{2,1,0:T(8,128)(2,1)} %pad_maximum_fusion.2), channel_id=1, source_target_pairs={{0,4},{4,0},{8,12},{12,8},{16,20},{20,16},{24,28},{28,24},{1,5},{5... | collective-permute-start | bytes 2359304 | tf_op jit(solution)/shard_map/while/body/eval_jaxpr/ppermute | solution.py:21
  1040.1 22.1 %copy-start.3 = (f32[768,768]{1,0:T(8,128)S(1)}, f32[768,768]{1,0:T(8,128)}, u32[]{:S(2)}) copy-start(f32[768,768]{1,0:T(8,128)} %get-tuple-element.1259) | copy-start | bytes 7077892 | tf_op jit(solution)/shard_map/while
  1040.1 22.1 %copy-start.13 = (bf16[768,1024]{1,0:T(8,128)(2,1)S(1)}, bf16[768,1024]{1,0:T(8,128)(2,1)}, u32[]{:S(2)}) copy-start(bf16[768,1024]{1,0:T(8,128)(2,1)} %all-gather.4.cloned.1.call-done) | copy-start | bytes 4718596 | tf_op jit(solution)/shard_map/while
  1060.6 35.8 %collective-permute-start.3 = (bf16[2,192,2048]{2,1,0:T(8,128)(2,1)S(1)}, bf16[2,192,2048]{2,1,0:T(8,128)(2,1)S(1)}, u32[]{:S(2)}, u32[]{:S(2)}) collective-permute-start(bf16[2,192,2048]{2,1,0:T(8,128)(2,1)S(1)} %maximum_select_fusion.22), channel_id=1, source_target_pairs={{0,8},{8,0},{4,12},{12,4},{16,24},{24,16},{20,28},{28,20},{1,9},{9... | collective-permute-start | bytes 4718600 | tf_op jit(solution)/shard_map/while/body/eval_jaxpr/ppermute | solution.py:21
  1062.2 3.6 copy-start.1
  1062.2 3.6 copy-start.14
  1062.2 3.6 copy-start.20
  1065.8 3.0 copy-start.4
  1068.7 28.8 %copy-start.2 = (f32[768,768]{1,0:T(8,128)}, f32[768,768]{1,0:T(8,128)S(1)}, u32[]{:S(2)}) copy-start(f32[768,768]{1,0:T(8,128)S(1)} %select_add_fusion.18) | copy-start | bytes 7077892 | tf_op jit(solution)/shard_map/while
  1097.8 64.3 %copy-start.17 = (f32[2,192,1024]{2,1,0:T(8,128)S(1)}, f32[2,192,1024]{2,1,0:T(8,128)}, u32[]{:S(2)}) copy-start(f32[2,192,1024]{2,1,0:T(8,128)} %get-tuple-element.1256) | copy-start | bytes 4718596 | tf_op jit(solution)/shard_map/while
  1225.4 1.1 copy-start.18
  1227.8 174.6 %all-reduce.16.cloned.1.call-start = ((), (), s32[]{:S(2)}) async-start(), calls=%async_computation.3 | async-start | bytes 9437184 | tf_op jit(solution)/shard_map/psum | solution.py:177
  1402.4 3.4 copy-start.5
Sparse Core Ops, SparseCore 0:
  185.8 39.0 reduce-scatter.15
  233.5 20.7 all-gather.3
  266.5 37.9 reduce-scatter.17
  321.6 21.1 all-gather.5
  358.2 37.9 reduce-scatter.19
  404.9 20.7 all-gather.7
  791.0 37.9 reduce-scatter.15
  837.6 20.7 all-gather.3
  870.6 37.9 reduce-scatter.17
  925.7 21.1 all-gather.5
  962.3 37.9 reduce-scatter.19
  1009.2 20.7 all-gather.7
Sparse Core Ops, SparseCore 1:
  1232.5 169.9 all-reduce.15
where the time goes:
time: 1420 us; the launch traced here: 1410 us
  waiting for transfers between devices  633 us (45%)
  matrix products  591 us (42%)
  blocking collectives  70.5 us (5%)
  other arithmetic  48.2 us (3%)
  local copies, waits for them, and re-layouts  37.2 us (3%)
  between operations  15.9 us (1%)
  starting transfers between devices  14.6 us (1%)
    dot_general x8, matrix products, product_left(): lax.dot_general(left, right, (((0,), (0,)), ((), ())), preferred_element_...  287 us
    dot_general x8, matrix products, product_right(): lax.dot_general(left, right, (((1,), (1,)), ((), ())), preferred_element_...  268 us
    psum x1, waiting for transfers between devices, local(): lax.psum((grads[0], grads[1], grads[2], grads[3], grads[4], grads[5], gra...  151 us
    ppermute x8, waiting for transfers between devices, from_partner(): return lax.ppermute(block, axis, route)  130 us
    reduce_scatter x2, waiting for transfers between devices, one_slot(): lax.psum_scatter(partial_value, 'hidden', scatter_dimension=0, tiled=True)  77.3 us
    reduce_scatter x2, waiting for transfers between devices, one_slot(): lax.psum_scatter(back_partial, 'hidden', scatter_dimension=0, tiled=True)  76.1 us
    reduce_scatter x2, waiting for transfers between devices, one_slot(): lax.psum_scatter(product_left(w_out, hidden_low), 'hidden', scatter_dimen...  74.8 us
    psum x8, blocking collectives, row_sums(): lax.psum((jnp.sum(first, 0, keepdims=True), jnp.sum(second, 0, keepdims=T...  47.3 us
  transfers between devices with their start and end apart: 21, of which 21 were waited for; matrix products, arithmetic and copies ran while one was open for 2% of the time, Pallas kernels for 0%

commit v1 on v0

v1 whole, which is shorter than its diff:
```python
import functools
import math

import jax
import jax.numpy as jnp
import ml_dtypes
import numpy as np
from jax import lax
from jax.experimental import pallas as pl
from jax.experimental.pallas import tpu as pltpu
from jax.sharding import PartitionSpec as P

SPLIT = 4
HOLD = 4
EPS = 1e-06
FINE = 64
LOW = jnp.bfloat16
F32 = jnp.float32
MESH = pl.DeviceIdType.MESH
VMEM_LIMIT = 58 * 2**20


def dot(left, right):
    return jnp.dot(left, right, preferred_element_type=F32)


def dot_rows(left, right):
    return lax.dot_general(left, right, (((1,), (1,)), ((), ())), preferred_element_type=F32)


@functools.cache
def sequence_tables(length, split):
    column = np.arange(length)
    coarse = 2 * np.pi * ((FINE * np.arange(length // FINE)[:, None] * column) % length) / length
    fine = 2 * np.pi * ((np.arange(FINE)[:, None] * column) % length) / length
    factor = 1 / math.sqrt(length)
    whole = np.stack([np.cos(coarse), np.sin(coarse), factor * np.cos(fine), factor * np.sin(fine)])
    return np.ascontiguousarray(
        whole.reshape(4, FINE, split, length // split).transpose(2, 0, 1, 3).astype(np.float32)
    )


@functools.cache
def feature_tables(width, parts):
    index = np.arange(width)
    angle = 2 * np.pi * ((index[:, None] * index) % width) / width
    factor = 1 / math.sqrt(width)
    cos = (np.cos(angle) * factor).astype(np.float32).astype(ml_dtypes.bfloat16)
    sin = (np.sin(angle) * factor).astype(np.float32).astype(ml_dtypes.bfloat16)
    part = width // parts
    pad = part + 16
    forward = np.zeros((parts, parts, part, 2 * part), ml_dtypes.bfloat16)
    backward = np.zeros((parts, pad, width), ml_dtypes.bfloat16)
    order = np.zeros((parts, part, pad), ml_dtypes.bfloat16)
    for h in range(parts):
        own = slice(h * part, (h + 1) * part)
        forward[h, :, :, :part] = cos[:, own].reshape(parts, part, part)
        forward[h, :, :, part:] = -sin[:, own].reshape(parts, part, part)
        first = (h // 2) * part
        backward[h, : part + 1] = (cos, sin)[h % 2][first : first + part + 1]
        for i in range(part):
            order[h, i, i if h in (0, 3) else part - i] = 1
    return forward, backward, order


class Place:
    def __init__(self):
        h = lax.axis_index("hidden")
        b = lax.axis_index("batch")
        self.h, self.b = h, b
        self.c = lax.rem(h, 2)
        self.x = lax.div(h, 2)
        self.hc = h + 1 - 2 * self.c
        self.hx = lax.rem(h + 2, 4)
        self.hd = lax.rem(self.hc + 2, 4)
        self.p = lax.rem(b, 4)
        y = lax.rem(b, 2)
        z = lax.div(self.p, 2)
        self.py = self.p + 1 - 2 * y
        self.pz = lax.rem(self.p + 2, 4)
        self.core = {"hidden": self.hc}
        self.side = {"hidden": self.hx}
        self.cross = {"hidden": self.hd}
        self.ydev = {"batch": b + 1 - 2 * y}
        self.zdev = {"batch": b + 2 - 4 * z}


class Links:
    def __init__(self, send, recv):
        self.send, self.recv, self.used, self.open = send, recv, 0, []

    def copy(self, src, dst, device):
        i = self.used
        self.used += 1
        made = pltpu.make_async_remote_copy(
            src_ref=src,
            dst_ref=dst,
            send_sem=self.send.at[i],
            recv_sem=self.recv.at[i],
            device_id=device,
            device_id_type=MESH,
        )
        made.start()
        self.open.append(made)
        return made

    def close(self):
        for made in self.open:
            made.wait_send()


def greet(devices):
    barrier = pltpu.get_barrier_semaphore()
    for device in devices:
        pl.semaphore_signal(barrier, inc=1, device_id=device, device_id_type=MESH)
    pl.semaphore_wait(barrier, len(devices))


class GatherHidden:
    def __init__(self, me, links, full):
        self.me, self.links, self.full = me, links, full

    def start_core(self):
        own = self.full.at[self.me.h]
        self.by_core = self.links.copy(own, own, self.me.core)

    def start_side(self):
        own = self.full.at[self.me.h]
        self.by_side = self.links.copy(own, own, self.me.side)

    def forward(self):
        self.by_side.wait_recv()
        far = self.full.at[self.me.hx]
        self.by_far = self.links.copy(far, far, self.me.core)


class GatherBatch:
    def __init__(self, me, links, full, cut):
        self.me, self.links, self.full, self.cut = me, links, full, cut

    def start(self):
        own = self.full.at[self.me.p]
        self.by_y = self.links.copy(own, own, self.me.ydev)
        self.by_z = self.links.copy(own, own, self.me.zdev)

    def forward(self):
        rows = self.full.shape[1]
        self.by_y.wait_recv()
        part = self.full.at[self.me.py, pl.ds(0, self.cut)]
        self.on_z = self.links.copy(part, part, self.me.zdev)
        self.by_z.wait_recv()
        part = self.full.at[self.me.pz, pl.ds(self.cut, rows - self.cut)]
        self.on_y = self.links.copy(part, part, self.me.ydev)

    def finish(self):
        self.on_z.wait_recv()
        self.on_y.wait_recv()


class Scatter:
    def __init__(self, me, links, sc, rc, sx, rx, acc, parts):
        self.me, self.links, self.parts = me, links, parts
        self.sc, self.rc, self.sx, self.rx, self.acc = sc, rc, sx, rx, acc

    def blocks(self):
        x, c = self.me.x, self.me.c
        far, near = 2 * (1 - x), 2 * x
        return far + 1 - c, far + c, near + 1 - c, near + c

    def run(self, block):
        for k, t in enumerate(self.blocks()):
            far, first = k < 2, k % 2 == 0
            n = 0 if far else 1

            def sink(i, value):
                if first:
                    self.sc[n, i] = value.astype(LOW)
                    return
                if i == 0:
                    self.by_core.wait_recv()
                value = value + self.rc[n, i].astype(F32)
                if far:
                    self.sx[i] = value.astype(LOW)
                else:
                    self.acc[i] = value

            block(t, sink)
            if first:
                self.by_core = self.links.copy(self.sc.at[n], self.rc.at[n], self.me.core)
            elif far:
                self.by_side = self.links.copy(self.sx, self.rx, self.me.side)

    def wait(self):
        self.by_side.wait_recv()

    def value(self, i):
        return self.acc[i] + self.rx[i].astype(F32)


def columns(t, size):
    return pl.ds(pl.multiple_of(t * size, size), size)


def mix_kernel(
    x_ref, cot_ref, live_ref, small_ref, ht_ref, r1_ref, ctok_ref,
    xg, tc, ts, cs, ct, ab, sc, rc, sx, rx, acc, send, recv,
):
    me = Place()
    slots, rows, piece = x_ref.shape
    tokens = piece // HOLD
    greet([me.core, me.side, me.cross, me.ydev, me.zdev])
    links = Links(send, recv)
    gathers = []
    for s in range(slots):
        xg[s, me.p] = x_ref[s].astype(LOW)
        gathers.append(GatherBatch(me, links, xg.at[s], rows // 2))
        if s == 0:
            gathers[0].start()
    moved = []
    for s in range(slots):
        for t in range(HOLD):
            cs[s, t] = (cot_ref[s, :, t * tokens : (t + 1) * tokens] * live_ref[s]).astype(LOW)
        ct[s, me.h] = cs[s, me.h]
        for to, device in ((me.hc, me.core), (me.hx, me.side), (me.hd, me.cross)):
            moved.append(links.copy(cs.at[s, to], ct.at[s, me.h], device))

    def make_rows(i, carry):
        big_cos, big_sin = small_ref[0, pl.ds(i, 1), :], small_ref[1, pl.ds(i, 1), :]
        at = pl.ds(pl.multiple_of(i * FINE, FINE), FINE)
        for n in range(piece // 256):
            cut = slice(n * 256, (n + 1) * 256)
            fine_cos, fine_sin = small_ref[2, :, cut], small_ref[3, :, cut]
            tc[at, cut] = (big_cos[:, cut] * fine_cos - big_sin[:, cut] * fine_sin).astype(LOW)
            ts[at, cut] = (big_sin[:, cut] * fine_cos + big_cos[:, cut] * fine_sin).astype(LOW)
        return carry

    lax.fori_loop(0, FINE, make_rows, 0)
    sums = [Scatter(me, links, sc.at[s], rc.at[s], sx.at[s], rx.at[s], acc.at[s], HOLD) for s in range(slots)]
    gathers[0].forward()
    for s in range(slots):
        gathers[s].finish()
        if s + 1 < slots:
            gathers[s + 1].start()

        def block(t, sink, s=s):
            at = columns(t, tokens)
            for part, table in ((0, tc), (1, ts)):
                total = dot(xg[s, 0], table[0:piece, at])
                for q in range(1, SPLIT):
                    total += dot(xg[s, q], table[q * piece : (q + 1) * piece, at])
                ab[part * rows : (part + 1) * rows, :] = total.astype(LOW)
            for i in range(HOLD):
                own = jnp.where(me.h == i, 1.0, 0.0).astype(F32)
                sink(i, dot(ht_ref[i], ab[...]) + own * x_ref[s, :, at])

        sums[s].run(block)
        if s + 1 < slots:
            gathers[s + 1].forward()
    for s in range(slots):
        sums[s].wait()
        for i in range(HOLD):
            r1_ref[s, i] = sums[s].value(i)
    for made in moved:
        made.wait_recv()
    ctok_ref[...] = ct[...]
    links.close()


ROOT = math.sqrt(2 / math.pi)
CUBE = 0.044715


def gelu_both(v):
    square = v * v
    t = jnp.tanh(v * (ROOT + ROOT * CUBE * square))
    half = 0.5 + 0.5 * t
    slope = half + (0.5 * v) * (1 - t * t) * (ROOT + 3 * ROOT * CUBE * square)
    return v * half, slope


def feed_kernel(
    r1_ref, ctok_ref, w1t_ref, w2t_ref, w1_ref, w2_ref, bin_ref, g1_ref, s1_ref, bo_ref, g2_ref, s2_ref,
    lo_ref, gm_ref, wg1_ref, wg2_ref, sg_ref,
    yf, hf, df, zf, y1, u1, gr2, inv1, lanes, sc, rc, sx, rx, acc, send, recv,
):
    me = Place()
    slots, parts, rows, tokens = r1_ref.shape
    width = parts * rows
    units = w1_ref.shape[1]
    steps = units // 256
    greet([me.core, me.side])
    links = Links(send, recv)

    def lane_sum(k, i, s, value):
        folded = value[:, :128] + value[:, 128:]
        lanes[k, i] = folded if s == 0 else lanes[k, i] + folded

    def up(value):
        return jnp.sum(value, 0, keepdims=True)

    def norm_first(s):
        total, squares = 0.0, 0.0
        for i in range(parts):
            v = r1_ref[s, i]
            total, squares = total + up(v), squares + up(v * v)
        mean = total / width
        inverse = lax.rsqrt(squares / width - mean * mean + EPS)
        inv1[s] = inverse
        for i in range(parts):
            u = (r1_ref[s, i] - mean) * inverse
            u1[s, i] = u
            y = u * g1_ref[i] + s1_ref[i]
            y1[s, i] = y
            yf[s, me.h, i * rows : (i + 1) * rows, :] = y.astype(LOW)

    def forward_in(s, t):
        for r in range(steps):
            at = slice(r * 256, (r + 1) * 256)
            h, slope = gelu_both(dot(w1t_ref[at, :], yf[s, t]) + bin_ref[at, :])
            hf[s, t, at, :] = h.astype(LOW)
            df[s, t, at, :] = slope.astype(LOW)

    def forward_out(s, t, sink):
        for i in range(parts):
            sink(i, dot(w2t_ref[i * rows : (i + 1) * rows, :], hf[s, t]))

    def norm_second(s, summed):
        total, squares = 0.0, 0.0
        for i in range(parts):
            v = y1[s, i] + summed.value(i) + bo_ref[i]
            summed.acc[i] = v
            total, squares = total + up(v), squares + up(v * v)
        mean = total / width
        inverse = lax.rsqrt(squares / width - mean * mean + EPS)
        total, cross = 0.0, 0.0
        for i in range(parts):
            u = (summed.acc[i] - mean) * inverse
            summed.acc[i] = u
            lo_ref[s, i] = (u * g2_ref[i] + s2_ref[i]).astype(LOW)
            g = ctok_ref[s, i].astype(F32)
            lane_sum(0, i, s, g * u)
            lane_sum(1, i, s, g)
            q = g * g2_ref[i]
            total, cross = total + up(q), cross + up(q * u)
        total, cross = total / width, cross / width
        for i in range(parts):
            q = ctok_ref[s, i].astype(F32) * g2_ref[i]
            grad = inverse * (q - total - summed.acc[i] * cross)
            gr2[s, i] = grad
            lane_sum(2, i, s, grad)
            zf[s, me.h, i * rows : (i + 1) * rows, :] = grad.astype(LOW)

    def backward_in(s, t, fresh):
        for r in range(steps):
            at = slice(r * 256, (r + 1) * 256)
            gp = dot(w2_ref[at, :], zf[s, t]) * df[s, t, at, :].astype(F32)
            folded = gp[:, :128] + gp[:, 128:]
            for n in range(256 // 64):
                cut = slice(n * 64, (n + 1) * 64)
                place = r * 256 + n * 64
                i, o = place // rows, place % rows
                lanes[5, i, o : o + 64] = folded[cut] if fresh else lanes[5, i, o : o + 64] + folded[cut]
            df[s, t, at, :] = gp.astype(LOW)

    def backward_out(s, t, sink):
        for i in range(parts):
            sink(i, dot(w1_ref[i * rows : (i + 1) * rows, :], df[s, t]))

    def weight_grads(s):
        def one(r, carry):
            at = columns(r, 256)
            for n in range(units // 256):
                cut = slice(n * 256, (n + 1) * 256)
                first, second = 0.0, 0.0
                for t in range(HOLD):
                    first = first + dot_rows(yf[s, t, at, :], df[s, t, cut, :])
                    second = second + dot_rows(hf[s, t, at, :], zf[s, t, cut, :])
                wg1_ref[at, cut] = first if s == 0 else wg1_ref[at, cut] + first
                wg2_ref[at, cut] = second if s == 0 else wg2_ref[at, cut] + second
            return carry

        lax.fori_loop(0, steps, one, 0)

    def norm_first_back(s, summed):
        total, cross = 0.0, 0.0
        for i in range(parts):
            grad = gr2[s, i] + summed.value(i)
            summed.acc[i] = grad
            u = u1[s, i]
            lane_sum(3, i, s, grad * u)
            lane_sum(4, i, s, grad)
            q = grad * g1_ref[i]
            total, cross = total + up(q), cross + up(q * u)
        total, cross = total / width, cross / width
        for i in range(parts):
            q = summed.acc[i] * g1_ref[i]
            gm_ref[s, i] = (inv1[s] * (q - total - u1[s, i] * cross)).astype(LOW)

    def scatter(s, way):
        n = 2 * way + s
        return Scatter(me, links, sc.at[n], rc.at[n], sx.at[n], rx.at[n], acc.at[n], parts)

    gathers = [GatherHidden(me, links, yf.at[s]) for s in range(slots)]
    sums = [scatter(s, 0) for s in range(slots)]
    for s in range(slots):
        norm_first(s)
        gathers[s].start_core()
        if s == 0:
            gathers[0].start_side()
    for s in range(slots):
        forward_in(s, me.h)
        gathers[s].by_core.wait_recv()
        forward_in(s, me.hc)
        gathers[s].forward()
        if s + 1 < slots:
            gathers[s + 1].start_side()
        forward_in(s, me.hx)
        gathers[s].by_far.wait_recv()
        forward_in(s, me.hd)
        sums[s].run(functools.partial(forward_out, s))
    gathers = [GatherHidden(me, links, zf.at[s]) for s in range(slots)]
    for s in range(slots):
        sums[s].wait()
        norm_second(s, sums[s])
        gathers[s].start_core()
        gathers[s].start_side()
    sums = [scatter(s, 1) for s in range(slots)]
    for s in range(slots):
        backward_in(s, me.h, s == 0)
        gathers[s].by_core.wait_recv()
        backward_in(s, me.hc, False)
        gathers[s].forward()
        backward_in(s, me.hx, False)
        gathers[s].by_far.wait_recv()
        backward_in(s, me.hd, False)
        sums[s].run(functools.partial(backward_out, s))
        weight_grads(s)
    for s in range(slots):
        sums[s].wait()
        norm_first_back(s, sums[s])
    lane = lax.broadcasted_iota(jnp.int32, (rows, 128), 1)
    for i in range(parts):
        packed = jnp.zeros((rows, 128), F32)
        for k in range(6):
            packed = jnp.where(lane == k, jnp.sum(lanes[k, i], 1, keepdims=True), packed)
        sg_ref[i] = packed
    links.close()


def back_kernel(
    gm_ref, lo_ref, live_ref, small_ref, gt_ref, order_ref, out_ref, grad_ref,
    gf, ug, og, tab, wv, ws, wr, rs, rr, send, recv,
):
    me = Place()
    slots, parts, rows, tokens = gm_ref.shape
    piece = parts * tokens
    width = parts * rows
    pad = gt_ref.shape[0]
    greet([me.core, me.side, me.cross, me.ydev, me.zdev])
    links = Links(send, recv)
    gathers = []
    for s in range(slots):
        gf[s, me.h] = gm_ref[s]
        gathers.append(GatherHidden(me, links, gf.at[s]))
        gathers[s].start_core()
        if s == 0:
            gathers[s].start_side()
    is_cos = me.c == 0

    def make_rows(i, carry):
        big_cos, big_sin = small_ref[0, pl.ds(i, 1), :], small_ref[1, pl.ds(i, 1), :]
        by_cos = jnp.where(is_cos, big_cos, big_sin)
        by_sin = jnp.where(is_cos, -big_sin, big_cos)
        at = pl.ds(pl.multiple_of(i * FINE, FINE), FINE)
        for n in range(piece // 256):
            cut = slice(n * 256, (n + 1) * 256)
            tab[at, cut] = (by_cos[:, cut] * small_ref[2, :, cut] + by_sin[:, cut] * small_ref[3, :, cut]).astype(LOW)
        return carry

    lax.fori_loop(0, FINE, make_rows, 0)
    spreads = [GatherBatch(me, links, ug.at[s], (pad // 32) * 16) for s in range(slots)]

    def features(s, t):
        whole = gf[s, t].reshape(width, tokens)
        ug[s, me.p, :, columns(t, tokens)] = dot(gt_ref[...], whole).astype(LOW)

    for s in range(slots):
        features(s, me.h)
        gathers[s].by_core.wait_recv()
        features(s, me.hc)
        gathers[s].forward()
        if s + 1 < slots:
            gathers[s + 1].start_side()
        features(s, me.hx)
        gathers[s].by_far.wait_recv()
        features(s, me.hd)
        if s > 0:
            spreads[s - 1].forward()
        spreads[s].start()
    moved = []
    for s in range(slots):
        og[s, me.h] = lo_ref[s, me.h]
        for to, device in ((me.hc, me.core), (me.hx, me.side), (me.hd, me.cross)):
            moved.append(links.copy(lo_ref.at[s, to], og.at[s, me.h], device))
    sign = jnp.where((me.h == 0) | (me.h == 3), -1.0, 1.0).astype(F32)
    mine = jnp.where(is_cos, 1.0, sign)
    theirs = jnp.where(is_cos, sign, 1.0)
    for s in range(slots):
        if s == slots - 1:
            spreads[s].forward()
        spreads[s].finish()
        for t in range(parts):
            at = slice(t * tokens, (t + 1) * tokens)
            total = dot(ug[s, 0], tab[0:piece, at])
            for q in range(1, SPLIT):
                total += dot(ug[s, q], tab[q * piece : (q + 1) * piece, at])
            wv[:, at] = total
            ws[s, :, at] = total.astype(LOW)
        swap = links.copy(ws.at[s], wr.at[s], me.core)
        swap.wait_recv()
        for t in range(parts):
            at = slice(t * tokens, (t + 1) * tokens)
            pair = (mine * wv[:, at] + theirs * wr[s, :, at].astype(F32)).astype(LOW)
            rs[s, :, at] = dot(order_ref[...], pair).astype(LOW)

        @pl.when(is_cos)
        def _(s=s):
            rr[s] = rs[s]

        @pl.when(jnp.logical_not(is_cos))
        def _(s=s):
            made = links.copy(rs.at[s], rr.at[s], me.side)
            links.open.pop()
            made.wait()

        for t in range(parts):
            at = slice(t * tokens, (t + 1) * tokens)
            grad_ref[s, :, at] = rr[s, :, at].astype(F32) + gf[s, t, me.h].astype(F32)
    for made in moved:
        made.wait_recv()
    for s in range(slots):
        for t in range(parts):
            out_ref[s, :, t * tokens : (t + 1) * tokens] = og[s, t].astype(F32) * live_ref[s]
    links.close()


def call(kernel, name, number, outs, scratch, smem, flops, *operands):
    specs = [
        pl.BlockSpec(memory_space=pltpu.SMEM if i in smem else pltpu.VMEM) for i in range(len(operands))
    ]
    return pl.pallas_call(
        kernel,
        name=name,
        out_shape=[jax.ShapeDtypeStruct(shape, kind) for shape, kind in outs],
        in_specs=specs,
        out_specs=[pl.BlockSpec(memory_space=pltpu.VMEM)] * len(outs),
        scratch_shapes=[pltpu.VMEM(shape, kind) for shape, kind in scratch]
        + [pltpu.SemaphoreType.DMA((64,)), pltpu.SemaphoreType.DMA((64,))],
        cost_estimate=pl.CostEstimate(flops=flops, bytes_accessed=16 * 2**20, transcendentals=0),
        compiler_params=pltpu.CompilerParams(
            collective_id=number, has_side_effects=True, vmem_limit_bytes=VMEM_LIMIT
        ),
    )(*operands)


def local(
    layer_input,
    gain_first,
    shift_first,
    weight_in,
    bias_in,
    weight_out,
    bias_out,
    gain_second,
    shift_second,
    cotangent,
    live_counts,
):
    slots, rows, piece = layer_input.shape
    width = rows * HOLD
    tokens = piece // HOLD
    units = weight_in.shape[1]
    length = piece * SPLIT
    pad = rows + 16
    hidden = lax.axis_index("hidden")
    position = lax.axis_index("batch") % SPLIT
    live = (jnp.arange(slots) < live_counts[0]).astype(F32)

    def pick(table, index):
        return lax.dynamic_index_in_dim(jnp.asarray(table), index, 0, keepdims=False)

    small = pick(sequence_tables(length, SPLIT), position)
    forward, backward, order = feature_tables(width, HOLD)
    forward, backward, order = pick(forward, hidden), pick(backward, hidden), pick(order, hidden)
    shard = (slots, HOLD, rows, tokens)
    whole = (slots, HOLD, width, tokens)
    r1, ctok = call(
        mix_kernel, "mix", 1, [(shard, F32), (shard, LOW)],
        [
            ((slots, SPLIT, rows, piece), LOW), ((length, piece), LOW), ((length, piece), LOW),
            (shard, LOW), (shard, LOW), ((2 * rows, tokens), LOW),
            ((slots, 2) + shard[1:], LOW), ((slots, 2) + shard[1:], LOW), (shard, LOW), (shard, LOW), (shard, F32),
        ],
        (2,), 4 * 10**9, layer_input, cotangent, live, small, forward,
    )

    w1, w2 = weight_in.astype(LOW), weight_out.astype(LOW)

    norms = jnp.stack([gain_first, shift_first, bias_out, gain_second, shift_second])
    norms = lax.all_gather(norms, "hidden", axis=0).transpose(1, 0, 2).reshape(5, HOLD, rows, 1)
    lo, gm, wg1, wg2, sg = call(
        feed_kernel, "feed", 2,
        [(shard, LOW), (shard, LOW), ((width, units), F32), ((units, width), F32), ((HOLD, rows, 128), F32)],
        [
            (whole, LOW), ((slots, HOLD, units, tokens), LOW), ((slots, HOLD, units, tokens), LOW), (whole, LOW),
            (shard, F32), (shard, F32), (shard, F32), ((slots, 1, tokens), F32), ((6, HOLD, rows, 128), F32),
            ((2 * slots, 2) + shard[1:], LOW), ((2 * slots, 2) + shard[1:], LOW),
            ((2 * slots,) + shard[1:], LOW), ((2 * slots,) + shard[1:], LOW), ((2 * slots,) + shard[1:], F32),
        ],
        (), 12 * 10**9, r1, ctok, w1.T, w2.T, w1, w2, bias_in.reshape(units, 1), *norms,
    )
    heavy = lax.psum(jnp.stack([wg1, wg2]).astype(LOW), "batch").astype(F32)
    sg = sg.reshape(width, 128)
    light = lax.psum_scatter(sg[:, :5].T.reshape(5, HOLD, rows), "hidden", scatter_dimension=1, tiled=False)
    light, bias_in_grad = lax.psum((light, sg[:, 5]), "batch")
    outputs, in_grads = call(
        back_kernel, "back", 3, [(layer_input.shape, F32), (layer_input.shape, F32)],
        [
            ((slots, HOLD) + shard[1:], LOW), ((slots, SPLIT, pad, piece), LOW), (shard, LOW), ((length, piece), LOW),
            ((pad, piece), F32), ((slots, pad, piece), LOW), ((slots, pad, piece), LOW),
            ((slots, rows, piece), LOW), ((slots, rows, piece), LOW),
        ],
        (2,), 4 * 10**9, gm, lo, live, small, backward, order,
    )
    return (
        outputs, in_grads, light[3], light[4], heavy[0], bias_in_grad, heavy[1], light[2], light[0], light[1],
    )


def solution(mesh):
    return jax.shard_map(
        local,
        mesh=mesh,
        in_specs=(
            P(None, "hidden", "batch"),
            P("hidden"),
            P("hidden"),
            P(None, "hidden"),
            P("hidden"),
            P("hidden", None),
            P("hidden"),
            P("hidden"),
            P("hidden"),
            P(None, "hidden", "batch"),
            P("batch"),
        ),
        out_specs=(
            P(None, "hidden", "batch"),
            P(None, "hidden", "batch"),
            P("hidden"),
            P("hidden"),
            P(None, "hidden"),
            P("hidden"),
            P("hidden", None),
            P("hidden"),
            P("hidden"),
            P("hidden"),
        ),
        check_vma=False,
    )
```

time: 1420 us -> 308 us (0.22)
  waiting for transfers between devices: 633 us -> 0.02 us
  matrix products: 591 us -> 0 us
  Pallas kernels: 0 us -> 197 us
  other arithmetic: 48.2 us -> 11.1 us
  blocking collectives: 70.5 us -> 55.1 us
  starting transfers between devices: 14.6 us -> 0.04 us
    dot_general x24 -> x0, matrix products: 591 us -> none  [the longest x8 287 us: product_left(): lax.dot_general(left, right, (((0,), (0,)), ((), ())), preferred_element_...]
    reduce_scatter x6 -> x0, waiting for transfers between devices: 228 us -> none  [the longest x2 77.3 us: one_slot(): lax.psum_scatter(partial_value, 'hidden', scatter_dimension=0, tiled=True)]
    pallas_call x0 -> x3, Pallas kernels: none -> 197 us  [call(): pl.pallas_call(kernel, name=name, out_shape=[jax.ShapeDtypeStruct(shape,...]
    psum x1, waiting for transfers between devices: 151 us -> 0.01 us  [local(): heavy = lax.psum(jnp.stack([wg1, wg2]).astype(LOW), 'batch').astype(F32)]
    ppermute x8 -> x0, waiting for transfers between devices: 130 us -> none  [from_partner(): return lax.ppermute(block, axis, route)]
    all_gather x6 -> x0, waiting for transfers between devices: 124 us -> none  [the longest x2 42.5 us: one_slot(): lax.all_gather(grad_second.astype(jnp.bfloat16), 'hidden', axis=0, tiled=...]
    psum x9 -> x1, blocking collectives: 70.5 us -> 38.3 us  [local(): light, bias_in_grad = lax.psum((light, sg[:, 5]), 'batch')]
    while x62 -> x0, local copies, waits for them, and re-layouts: 29.5 us -> none
  transfers between devices with their start and end apart: 21 -> 1, of which waited for: 21 -> 0; matrix products, arithmetic and copies ran while one was open for 2% -> 2% of each run, Pallas kernels for 0% -> 21%
where the time goes in v1:
time: 308 us; the launch traced here: 305 us
  Pallas kernels  197 us (64%)
  blocking collectives  55.1 us (18%)
  local copies, waits for them, and re-layouts  26.3 us (9%)
  between operations  15.3 us (5%)
  other arithmetic  11.1 us (4%)
    pallas_call x3, Pallas kernels, call(): pl.pallas_call(kernel, name=name, out_shape=[jax.ShapeDtypeStruct(shape,...  197 us
    psum x1, blocking collectives, local(): light, bias_in_grad = lax.psum((light, sg[:, 5]), 'batch')  38.3 us
    unnamed x1, blocking collectives  10.7 us
    squeeze x4, local copies, waits for them, and re-layouts, pick(): lax.dynamic_index_in_dim(jnp.asarray(table), index, 0, keepdims=False)  7.52 us
    unnamed x30, local copies, waits for them, and re-layouts  6.83 us
    all_gather x1, blocking collectives, local(): lax.all_gather(norms, 'hidden', axis=0).transpose(1, 0, 2)  6.17 us
  transfers between devices with their start and end apart: 1, of which 0 were waited for; matrix products, arithmetic and copies ran while one was open for 2% of the time, Pallas kernels for 21%

profile of v1, /device:TPU:0, one launch (start us, length us, event | category | flops | bytes accessed | tf_op | source)
XLA Modules:
  0.0 305.1 jit_solution(8129626331803105010)
XLA Ops:
  7.2 0.0 copy-start
  7.2 0.0 all-reduce.4.cloned.1.call-start
  7.2 1.9 convert_bitcast_fusion.3
  9.2 0.4 copy-done
  9.6 0.0 copy-start.1
  9.6 1.1 convert_element_type.14.w1_ref
  10.7 1.0 copy-done.1
  11.6 0.1 convert_bitcast_fusion.2
  11.8 0.0 copy-start.6
  11.8 0.0 copy-start.7
  11.8 0.0 copy-start.8
  11.8 0.0 copy-start.9
  11.8 0.0 copy-start.10
  11.8 1.1 convert_element_type.15.w2_ref
  13.6 0.5 compare_convert_fusion.live_ref
  14.1 0.0 copy-done.6
  14.1 0.0 copy-done.7
  14.1 0.0 copy-done.8
  14.1 0.0 copy-done.9
  14.1 0.0 copy-done.10
  14.2 6.2 %all-gather.1 = f32[4,5,192]{2,1,0:T(8,128)S(1)} all-gather(f32[1,5,192]{2,1,0:T(8,128)S(1)} %bitcast.47), channel_id=2, replica_groups=mesh['batch'=8,'hidden'=4] {'hidden'}, dimensions={0}, use_global_device_ids=true | all-gather | bytes 19200 | tf_op jit(solution)/shard_map/all_gather | solution.py:610
  20.3 0.1 slice_reduce_fusion.1
  20.4 0.9 unstack.40.g1_ref
  21.3 0.9 unstack.41.s1_ref
  22.3 0.9 unstack.42.bo_ref
  23.2 0.9 unstack.43.g2_ref
  24.1 0.9 unstack.44.s2_ref
  25.0 0.0 copy-start.5
  25.0 1.4 copy.76.w1t_ref
  26.5 1.4 copy.77.w2t_ref
  27.9 0.0 copy-done.5
  27.9 0.9 reshape.50.bin_ref
  28.8 2.3 dynamic-slice_bitcast_fusion.small_ref
  31.2 1.9 dynamic-slice_bitcast_fusion.1.ht_ref
  33.1 51.7 %mix.1 = (f32[2,4,192,256]{3,2,1,0:T(8,128)}, bf16[2,4,192,256]{3,2,1,0:T(8,128)(2,1)}) custom-call(f32[2,192,1024]{2,1,0:T(8,128)} %x_ref.1, f32[2,192,1024]{2,1,0:T(8,128)} %cot_ref.1, f32[2]{0:T(128)} %compare_convert_fusion.live_ref, f32[4,64,1024]{2,1,0:T(8,128)} %dynamic-slice_bitcast_fusion.small_ref, ...), custom_call_target="tpu_custom_call" | custom-call | flops 4000000000 | bytes 16777216 | tf_op jit(solution)/shard_map/mix/pallas_call | solution.py:551
  84.8 82.4 %feed.1 = (bf16[2,4,192,256]{3,2,1,0:T(8,128)(2,1)}, bf16[2,4,192,256]{3,2,1,0:T(8,128)(2,1)}, f32[768,768]{1,0:T(8,128)}, f32[768,768]{1,0:T(8,128)}, f32[4,192,128]{2,1,0:T(8,128)}) custom-call(f32[2,4,192,256]{3,2,1,0:T(8,128)} %get-tuple-element.19.r1_ref, bf16[2,4,192,256]{3,2,1,0:T(8,128)(2,1)} %get-tuple-element.20.ctok_ref, ...), custom_call_target="tpu_custom_call" | custom-call | flops 12000000000 | bytes 16777216 | tf_op jit(solution)/shard_map/feed/pallas_call | solution.py:551
  167.2 2.6 convert_bitcast_fusion
  169.8 1.6 pad_maximum_fusion
  171.4 0.0 copy-start.4
  171.4 0.0 copy-start.11
  171.4 0.0 all-reduce.4.cloned.1.call-update
  171.5 1.0 copy-done.4
  172.4 0.1 copy.89
  172.6 0.1 reshape.42
  172.7 0.0 copy-done.11
  172.7 0.6 dynamic-slice
  173.3 10.7 %all-reduce = f32[5,4,192]{2,1,0:T(4,128)S(1)} all-reduce(f32[5,4,192]{2,1,0:T(4,128)S(1)} %reshape.42), channel_id=3, replica_groups=mesh['batch'=8,'hidden'=4] {'hidden'}, use_global_device_ids=true, to_apply=%region_0.1.clone | all-reduce | flops 3840 | bytes 30720
  183.9 0.7 constant_dynamic-slice_fusion
  184.6 1.5 dynamic-slice_bitcast_fusion.3.order_ref
  186.2 1.7 dynamic-slice_bitcast_fusion.2.gt_ref
  187.9 63.2 %back.1 = (f32[2,192,1024]{2,1,0:T(8,128)}, f32[2,192,1024]{2,1,0:T(8,128)}) custom-call(bf16[2,4,192,256]{3,2,1,0:T(8,128)(2,1)} %get-tuple-element.21.gm_ref, bf16[2,4,192,256]{3,2,1,0:T(8,128)(2,1)} %get-tuple-element.22.lo_ref, f32[2]{0:T(128)} %compare_convert_fusion.live_ref, f32[4,64,1024]{2,1,0:T(8,128)} %dynamic-slice_bitcast_fusion.small_ref, ...), custom_call_target="tpu_custom_call" | custom-call | flops 4000000000 | bytes 16777216 | tf_op jit(solution)/shard_map/back/pallas_call | solution.py:551
  251.0 0.3 slice_reduce_fusion
  251.3 38.3 %all-reduce.1 = (f32[5,192]{1,0:T(8,128)S(1)}, f32[768]{0:T(1024)}) all-reduce(f32[5,192]{1,0:T(8,128)S(1)} %bitcast.48, f32[768]{0:T(1024)S(1)} %slice_reduce_fusion), channel_id=1, replica_groups=mesh['batch'=8,'hidden'=4] {'batch'}, use_global_device_ids=true, to_apply=%region_1.2 | all-reduce | flops 1728 | bytes 13824 | tf_op jit(solution)/shard_map/psum | solution.py:625
  289.6 0.6 fusion
  290.2 0.0 all-reduce.4.cloned.1.call-done
  290.2 2.0 convert_element_type.16
  292.2 0.0 copy-start.3
  292.3 2.5 slice_bitcast_fusion
  294.7 0.0 copy-start.2
  294.7 0.0 copy-done.3
  294.7 1.1 copy.98
  295.9 0.8 copy-done.2
  296.7 1.1 copy.99
  (2 shorter events, 0.0 us)
Async XLA Ops:
  7.2 2.4 copy-start
  7.2 283.0 %all-reduce.4.cloned.1.call-start = ((), (), s32[]{:S(2)}) async-start(), calls=%async_computation | async-start | bytes 4718592 | tf_op jit(solution)/shard_map/psum | solution.py:622
  9.6 2.1 copy-start.1
  11.8 2.4 copy-start.6
  11.8 2.3 copy-start.7
  11.8 2.3 copy-start.8
  11.8 2.3 copy-start.9
  11.8 2.3 copy-start.10
  25.0 2.9 copy-start.5
  171.4 1.0 copy-start.4
  171.4 1.2 copy-start.11
  292.2 2.5 copy-start.3
  294.7 2.0 copy-start.2
Sparse Core Ops, SparseCore 0:
  171.6 114.8 all-reduce.3
